TPU v7x, 32 devices: a whole 2x2x4 slice. The times are simulated.
32 devices in a mesh: section: 4 (over z), expert: 4 (over y, x), dp: 2 (over core).
Axes of the slice: x: 2, y: 2, z: 4, core: 2. Of those that a mesh axis runs over, the one named last changes fastest.
Arguments:
- acts: bfloat16 [4, 3, 512, 1024], P('section', None, ('expert', 'dp')), may hold values from -6 to 6
- out_grad: bfloat16 [3, 512, 1024], P(None, ('expert', 'dp')), may hold values from -6 to 6
- ln_gain: float32 [4, 1024], P('section'), may hold values from 0.1 to 1.9
- router: bfloat16 [4, 1024, 4], P('section'), may hold values from -0.1875 to 0.1875
- w_in: bfloat16 [4, 4, 1024, 4096], P('section', 'expert', None, 'dp'), may hold values from -0.1875 to 0.1875
- w_out: bfloat16 [4, 4, 4096, 1024], P('section', 'expert', 'dp'), may hold values from -0.09375 to 0.09375
- expert_ids: int32 [4, 3, 512, 2], P('section', None, ('expert', 'dp')), may hold values from 0 to 3, as said below
- slot_ids: int32 [4, 3, 512, 2], P('section', None, ('expert', 'dp')), may hold values from 0 to 39, as said below
- capacity: int32 [4, 3, 4], P('section'), may hold values from 20 to 40
Outputs:
- in_grads: bfloat16 [4, 3, 512, 1024], P('section', None, ('expert', 'dp'))
- gain_grad: float32 [4, 1024], P('section')
- router_grad: float32 [4, 1024, 4], P('section')
Inputs may be any that keep to these rules, and one draw needn't show every extreme that they name: `expert_ids`: A token's two experts differ. `slot_ids`: within one block, micro-batch and aligned block of 64 tokens (the tokens of one device), the choices that name one expert hold the slots 0, 1, 2, ... without gaps, at most 40 of them; in every block and micro-batch one expert has 40 choices from every aligned block and capacity 40.
All inputs are finite; a program needn't handle non-finite values.
Results may differ from a plain program's by a relative error of at most 0.03.
Values may be sent and summed in bfloat16 or wider, within the bound.
No kernel may reach another device: no remote copies, remote signals or barrier semaphores. Data moves between devices by JAX's collectives and lax.ppermute only.
A program may use at most 128 MiB of HBM per device.

v0:
```python
import math

import jax
import jax.numpy as jnp
from jax import lax
from jax.sharding import PartitionSpec as P

GELU_C = math.sqrt(2.0 / math.pi)
PRECISE = lax.Precision.HIGHEST


def from_behind(shard, axis, by):
    count = lax.axis_size(axis)
    pairs = [(i, i + by) for i in range(count) if 0 <= i + by < count]
    return lax.ppermute(shard, axis, pairs)


def gelu_pair(hidden):
    inner_arg = GELU_C * (hidden + 0.044715 * hidden * hidden * hidden)
    tanh_val = jnp.tanh(inner_arg)
    active = 0.5 * hidden * (1.0 + tanh_val)
    gelu_slope = 0.5 * (1.0 + tanh_val) + 0.5 * hidden * (1.0 - tanh_val * tanh_val) * GELU_C * (
        1.0 + 3.0 * 0.044715 * hidden * hidden
    )
    return (active, gelu_slope)


def token_forward(inputs, norm_scale_weight, router_w):
    values = inputs.astype(jnp.float32)
    centred = values - jnp.mean(values, axis=-1, keepdims=True)
    inverse_deviation = lax.rsqrt(jnp.mean(centred * centred, axis=-1, keepdims=True) + 1e-06)
    expert_unit_rows = centred * inverse_deviation
    normed = (expert_unit_rows * norm_scale_weight).astype(jnp.bfloat16)
    logits = jnp.dot(normed, router_w, preferred_element_type=jnp.float32)
    return (expert_unit_rows, inverse_deviation, normed, logits)


def gate_pair(chosen):
    first_gate = 1.0 / (1.0 + jnp.exp(chosen[:, 1] - chosen[:, 0]))
    return jnp.stack([first_gate, 1.0 - first_gate], axis=1)


def token_backward(
    grad_out,
    expert_unit_rows,
    inverse_deviation,
    normed,
    norm_scale_weight,
    router_w,
    gate_vals,
    pick_table,
    gate_dots,
    expert_part,
):
    gate_diff = gate_vals[:, 0] * gate_vals[:, 1] * (gate_dots[:, 0] - gate_dots[:, 1])
    dlogits = gate_diff[:, None] * (pick_table[:, 0, :] - pick_table[:, 1, :])
    norm_gradient = expert_part + jnp.dot(
        dlogits, router_w.astype(jnp.float32).T, precision=PRECISE
    )
    router_term = jnp.dot(normed.astype(jnp.float32).T, dlogits, precision=PRECISE)
    gain_term = jnp.sum(norm_gradient * expert_unit_rows, axis=0)
    normalized_input_gradient = norm_gradient * norm_scale_weight
    input_gradient = inverse_deviation * (
        normalized_input_gradient
        - jnp.mean(normalized_input_gradient, axis=-1, keepdims=True)
        - expert_unit_rows
        * jnp.mean(normalized_input_gradient * expert_unit_rows, axis=-1, keepdims=True)
    )
    in_grad = (grad_out.astype(jnp.float32) + input_gradient).astype(jnp.bfloat16)
    return (in_grad, gain_term, router_term)


def expert_terms(rows_u, rows_grad, first_proj, second_proj):
    hidden = jnp.dot(rows_u, first_proj, preferred_element_type=jnp.float32)
    active, gelu_slope = gelu_pair(hidden)
    back_grad = lax.dot_general(
        rows_grad, second_proj, (((1,), (1,)), ((), ())), preferred_element_type=jnp.float32
    )
    gate_part = jnp.sum(active * back_grad, axis=-1)
    pre_grad = (back_grad * gelu_slope).astype(jnp.bfloat16)
    slot_part = lax.dot_general(
        pre_grad, first_proj, (((1,), (1,)), ((), ())), preferred_element_type=jnp.float32
    )
    return (slot_part, gate_part)


def per_device(acts, out_grad, ln_gain, router, w_in, w_out, expert_ids, slot_ids, capacity):
    section_count = lax.axis_size("section")
    section_index = lax.axis_index("section")
    microbatch_count = acts.shape[1]
    tok_rows = acts.shape[2]
    model_width = acts.shape[3]
    experts = router.shape[2]
    top_count = expert_ids.shape[3]
    cap_slots = 5 * tok_rows * top_count // (4 * experts)
    slot_count = experts * cap_slots
    tokens_all = tok_rows * lax.axis_size("expert") * lax.axis_size("dp")
    grad_scale = 1.0 / math.sqrt(microbatch_count * tokens_all)
    norm_scale_weight = ln_gain[0]
    router_w = router[0]
    first_proj = w_in[0, 0]
    second_proj = w_out[0, 0]
    positions = jnp.arange(slot_count, dtype=jnp.int32)
    columns = jnp.arange(experts, dtype=jnp.int32)
    section_acts = acts[0]
    section_ids = expert_ids[0]
    section_slots = slot_ids[0]
    section_caps = capacity[0]

    def run_experts(recv_u, recv_grad, is_valid):
        lead_rows = recv_u.shape[0]
        flat_u = recv_u.reshape(lead_rows * cap_slots, model_width)
        flat_grad = recv_grad.reshape(lead_rows * cap_slots, model_width)

        def expert_work(packed):
            return expert_terms(packed[0], packed[1], first_proj, second_proj)

        def skip_work(packed):
            return (
                jnp.zeros(packed[0].shape, jnp.float32),
                jnp.zeros(packed[0].shape[:1], jnp.float32),
            )

        slot_part, gate_part = lax.cond(is_valid, expert_work, skip_work, (flat_u, flat_grad))
        return (
            slot_part.reshape(lead_rows, cap_slots, model_width),
            gate_part.reshape(lead_rows, cap_slots),
        )

    def step_fn(step_index, loop_state):
        incoming, grads_acc, gain_acc, router_acc = loop_state
        micro_index = step_index - (section_count - 1 - section_index)
        is_valid = jnp.logical_and(micro_index >= 0, micro_index < microbatch_count)
        picked = jnp.clip(micro_index, 0, microbatch_count - 1)
        last_grad = lax.dynamic_index_in_dim(out_grad, picked, 0, keepdims=False)
        grad_out = jnp.where(section_index == section_count - 1, last_grad, incoming)
        inputs_now = lax.dynamic_index_in_dim(section_acts, picked, 0, keepdims=False)
        ids_now = lax.dynamic_index_in_dim(section_ids, picked, 0, keepdims=False)
        slots_now = lax.dynamic_index_in_dim(section_slots, picked, 0, keepdims=False)
        caps_now = lax.dynamic_index_in_dim(section_caps, picked, 0, keepdims=False)
        expert_unit_rows, inverse_deviation, normed, logits = token_forward(
            inputs_now, norm_scale_weight, router_w
        )
        pick_bool = ids_now[:, :, None] == columns
        pick_table = pick_bool.astype(jnp.float32)
        chosen = jnp.sum(pick_table * logits[:, None, :], axis=2)
        gate_vals = gate_pair(chosen)
        cap_sel = jnp.sum(jnp.where(pick_bool, caps_now, 0), axis=2)
        kept_mask = slots_now < cap_sel
        target = jnp.where(kept_mask, ids_now * cap_slots + slots_now, -1)
        send_map = jnp.any(positions[:, None, None] == target[None, :, :], axis=2).astype(
            jnp.bfloat16
        )
        sent_u = (
            jnp.dot(send_map, normed, preferred_element_type=jnp.float32)
            .astype(jnp.bfloat16)
            .reshape(experts, cap_slots, model_width)
        )
        sent_grad = (
            jnp.dot(send_map, grad_out, preferred_element_type=jnp.float32)
            .astype(jnp.bfloat16)
            .reshape(experts, cap_slots, model_width)
        )
        recv_u, recv_grad = (
            lax.all_to_all(sent_u, "expert", split_axis=0, concat_axis=0, tiled=True),
            lax.all_to_all(sent_grad, "expert", split_axis=0, concat_axis=0, tiled=True),
        )
        both_u, both_grad = (
            lax.all_gather(recv_u, "dp", axis=0, tiled=True),
            lax.all_gather(recv_grad, "dp", axis=0, tiled=True),
        )
        slot_part, gate_part = run_experts(both_u, both_grad, is_valid)
        summed_u, summed_g = (
            lax.psum_scatter(slot_part, "dp", scatter_dimension=0, tiled=True),
            lax.psum_scatter(gate_part, "dp", scatter_dimension=0, tiled=True),
        )
        ret_u, ret_g = (
            lax.all_to_all(
                summed_u.astype(jnp.bfloat16), "expert", split_axis=0, concat_axis=0, tiled=True
            ),
            lax.all_to_all(
                summed_g.astype(jnp.bfloat16), "expert", split_axis=0, concat_axis=0, tiled=True
            ),
        )
        flat_ret = ret_u.reshape(slot_count, model_width).astype(jnp.float32)
        flat_gate = ret_g.reshape(slot_count).astype(jnp.float32)
        hit_table = (target[:, :, None] == positions).astype(jnp.float32)
        mix_table = jnp.sum(hit_table * gate_vals[:, :, None], axis=1)
        expert_part = jnp.dot(mix_table, flat_ret, precision=PRECISE)
        gate_dots = jnp.sum(hit_table * flat_gate, axis=2)
        in_grad, gain_term, router_term = token_backward(
            grad_out,
            expert_unit_rows,
            inverse_deviation,
            normed,
            norm_scale_weight,
            router_w,
            gate_vals,
            pick_table,
            gate_dots,
            expert_part,
        )
        grads_acc = jnp.where(
            is_valid, lax.dynamic_update_index_in_dim(grads_acc, in_grad, picked, 0), grads_acc
        )
        gain_acc = gain_acc + jnp.where(is_valid, gain_term, 0.0)
        router_acc = router_acc + jnp.where(is_valid, router_term, 0.0)
        outgoing = from_behind(in_grad, "section", -1)
        return (outgoing, grads_acc, gain_acc, router_acc)

    start_state = (
        jnp.zeros((tok_rows, model_width), jnp.bfloat16),
        jnp.zeros((microbatch_count, tok_rows, model_width), jnp.bfloat16),
        jnp.zeros((model_width,), jnp.float32),
        jnp.zeros((model_width, experts), jnp.float32),
    )
    final_state = lax.fori_loop(0, microbatch_count + section_count - 1, step_fn, start_state)
    grads_acc = final_state[1]
    gain_acc, router_acc = (
        lax.psum(final_state[2].astype(jnp.bfloat16), ("expert", "dp")).astype(jnp.float32),
        lax.psum(final_state[3].astype(jnp.bfloat16), ("expert", "dp")).astype(jnp.float32),
    )
    return (grads_acc[None], (gain_acc * grad_scale)[None], (router_acc * grad_scale)[None])


def solution(mesh):
    return jax.shard_map(
        per_device,
        mesh=mesh,
        in_specs=(
            P("section", None, ("expert", "dp"), None),
            P(None, ("expert", "dp"), None),
            P("section", None),
            P("section", None, None),
            P("section", "expert", None, "dp"),
            P("section", "expert", "dp", None),
            P("section", None, ("expert", "dp"), None),
            P("section", None, ("expert", "dp"), None),
            P("section", None, None),
        ),
        out_specs=(
            P("section", None, ("expert", "dp"), None),
            P("section", None),
            P("section", None, None),
        ),
        check_vma=False,
    )
```

profile of v0, /device:TPU:0, one launch (start us, length us, event | category | flops | bytes accessed | tf_op | source)
XLA Modules:
  0.0 449.3 jit_solution(3350281904756731496)
XLA Ops:
  7.9 411.0 %while.23 = (s32[]{:T(128)}, bf16[64,1024]{1,0:T(8,128)(2,1)S(1)}, bf16[3,64,1024]{2,1,0:T(8,128)(2,1)S(1)}, f32[1024]{0:T(1024)S(1)}, f32[1024,4]{0,1:T(4,128)S...) while((s32[]{:T(128)}, bf16[64,1024]{1,0:T(8,128)(2,1)S(1)}, ...), condition=%wide.region_16.17_spmd.clone.clone, body=%wide.region_0.16_spmd.clone.clone.sunk | while | flops 4223709696 | bytes 85165424 | solution.py:217
  13.7 5.2 %all-to-all-start.1 = ((bf16[4,40,1024]{2,1,0:T(8,128)(2,1)}), bf16[4,40,1024]{2,1,0:T(8,128)(2,1)S(1)}, u32[]{:S(2)}, u32[]{:S(2)}) async-start(bf16[4,40,1024]{2,1,0:T(8,128)(2,1)} %bitcast.159), calls=%async_computation.1 | async-start | bytes 655360 | tf_op jit(solution)/shard_map/while/body/eval_jaxpr/all_to_all | solution.py:165
  45.9 4.5 %all-to-all-done.2 = bf16[4,1,40]{2,1,0:T(2,128)(2,1)S(1)} async-done(((bf16[4,1,40]{2,1,0:T(2,128)(2,1)}), bf16[4,1,40]{2,1,0:T(2,128)(2,1)S(1)}, u32[]{:S(2)}, u32[]{:S(2)}) %all-to-all-start.2) | async-done | bytes 352 | tf_op jit(solution)/shard_map/while/body/eval_jaxpr/all_to_all | solution.py:181
  61.4 5.7 %all-to-all-done.3 = bf16[4,40,1024]{2,1,0:T(8,128)(2,1)S(1)} async-done(((bf16[4,40,1024]{2,1,0:T(8,128)(2,1)}), bf16[4,40,1024]{2,1,0:T(8,128)(2,1)S(1)}, u32[]{:S(2)}, u32[]{:S(2)}) %all-to-all-start.3) | async-done | bytes 327712 | tf_op jit(solution)/shard_map/while/body/eval_jaxpr/all_to_all | solution.py:178
  69.9 5.5 %collective-permute-done = bf16[64,1024]{1,0:T(8,128)(2,1)S(1)} collective-permute-done((bf16[64,1024]{1,0:T(8,128)(2,1)S(1)}, bf16[64,1024]{1,0:T(8,128)(2,1)S(1)}, u32[]{:S(2)}, u32[]{:S(2)}) %collective-permute-start) | collective-permute-done | bytes 131104 | tf_op jit(solution)/shard_map/while/body/eval_jaxpr/ppermute | solution.py:15
  111.3 4.5 %all-to-all-done.2 = bf16[4,1,40]{2,1,0:T(2,128)(2,1)S(1)} async-done(((bf16[4,1,40]{2,1,0:T(2,128)(2,1)}), bf16[4,1,40]{2,1,0:T(2,128)(2,1)S(1)}, u32[]{:S(2)}, u32[]{:S(2)}) %all-to-all-start.2) | async-done | bytes 352 | tf_op jit(solution)/shard_map/while/body/eval_jaxpr/all_to_all | solution.py:181
  116.1 5.2 %reduce-scatter.2.cloned.1.call-done = f32[4,40,1024]{2,1,0:T(8,128)} async-done(((f32[8,40,1024]{2,1,0:T(8,128)}), f32[4,40,1024]{2,1,0:T(8,128)}) %reduce-scatter.2.cloned.1.call-update) | async-done | bytes 655376 | tf_op jit(solution)/shard_map/while/body/eval_jaxpr/reduce_scatter | solution.py:174
  127.8 5.7 %all-to-all-done.3 = bf16[4,40,1024]{2,1,0:T(8,128)(2,1)S(1)} async-done(((bf16[4,40,1024]{2,1,0:T(8,128)(2,1)}), bf16[4,40,1024]{2,1,0:T(8,128)(2,1)S(1)}, u32[]{:S(2)}, u32[]{:S(2)}) %all-to-all-start.3) | async-done | bytes 327712 | tf_op jit(solution)/shard_map/while/body/eval_jaxpr/all_to_all | solution.py:178
  136.3 5.5 %collective-permute-done = bf16[64,1024]{1,0:T(8,128)(2,1)S(1)} collective-permute-done((bf16[64,1024]{1,0:T(8,128)(2,1)S(1)}, bf16[64,1024]{1,0:T(8,128)(2,1)S(1)}, u32[]{:S(2)}, u32[]{:S(2)}) %collective-permute-start) | collective-permute-done | bytes 131104 | tf_op jit(solution)/shard_map/while/body/eval_jaxpr/ppermute | solution.py:15
  177.7 4.5 %all-to-all-done.2 = bf16[4,1,40]{2,1,0:T(2,128)(2,1)S(1)} async-done(((bf16[4,1,40]{2,1,0:T(2,128)(2,1)}), bf16[4,1,40]{2,1,0:T(2,128)(2,1)S(1)}, u32[]{:S(2)}, u32[]{:S(2)}) %all-to-all-start.2) | async-done | bytes 352 | tf_op jit(solution)/shard_map/while/body/eval_jaxpr/all_to_all | solution.py:181
  182.5 7.3 %reduce-scatter.2.cloned.1.call-done = f32[4,40,1024]{2,1,0:T(8,128)} async-done(((f32[8,40,1024]{2,1,0:T(8,128)}), f32[4,40,1024]{2,1,0:T(8,128)}) %reduce-scatter.2.cloned.1.call-update) | async-done | bytes 655376 | tf_op jit(solution)/shard_map/while/body/eval_jaxpr/reduce_scatter | solution.py:174
  196.2 5.7 %all-to-all-done.3 = bf16[4,40,1024]{2,1,0:T(8,128)(2,1)S(1)} async-done(((bf16[4,40,1024]{2,1,0:T(8,128)(2,1)}), bf16[4,40,1024]{2,1,0:T(8,128)(2,1)S(1)}, u32[]{:S(2)}, u32[]{:S(2)}) %all-to-all-start.3) | async-done | bytes 327712 | tf_op jit(solution)/shard_map/while/body/eval_jaxpr/all_to_all | solution.py:178
  204.8 8.7 %collective-permute-done = bf16[64,1024]{1,0:T(8,128)(2,1)S(1)} collective-permute-done((bf16[64,1024]{1,0:T(8,128)(2,1)S(1)}, bf16[64,1024]{1,0:T(8,128)(2,1)S(1)}, u32[]{:S(2)}, u32[]{:S(2)}) %collective-permute-start) | collective-permute-done | bytes 131104 | tf_op jit(solution)/shard_map/while/body/eval_jaxpr/ppermute | solution.py:15
  239.4 8.7 %conditional.4 = (f32[320,1024]{1,0:T(8,128)S(1)}, f32[320]{0:T(512)S(1)}) conditional(s32[]{:T(128)} %convert_element_type.282, () %tuple.78, (bf16[8,40,1024]{2,1,0:T(8,128)(2,1)S(1)}, bf16[2048,1024]{1,0:T(8,128)(2,1)}, bf16[8,40,1024]{2,1,0:T(8,128)(2,1)S(1)}, bf16[1024,2048]{1,0:T(8,128)(2,1)}) %tuple.79), branch_computations={%region_7.7_spmd, %region_8.9_spmd} | conditional | flops 4045537024 | bytes 61867336 | solution.py:124
  257.9 4.5 %all-to-all-done.2 = bf16[4,1,40]{2,1,0:T(2,128)(2,1)S(1)} async-done(((bf16[4,1,40]{2,1,0:T(2,128)(2,1)}), bf16[4,1,40]{2,1,0:T(2,128)(2,1)S(1)}, u32[]{:S(2)}, u32[]{:S(2)}) %all-to-all-start.2) | async-done | bytes 352 | tf_op jit(solution)/shard_map/while/body/eval_jaxpr/all_to_all | solution.py:181
  268.7 4.9 %all-to-all-done.3 = bf16[4,40,1024]{2,1,0:T(8,128)(2,1)S(1)} async-done(((bf16[4,40,1024]{2,1,0:T(8,128)(2,1)}), bf16[4,40,1024]{2,1,0:T(8,128)(2,1)S(1)}, u32[]{:S(2)}, u32[]{:S(2)}) %all-to-all-start.3) | async-done | bytes 327712 | tf_op jit(solution)/shard_map/while/body/eval_jaxpr/all_to_all | solution.py:178
  276.4 5.5 %collective-permute-done = bf16[64,1024]{1,0:T(8,128)(2,1)S(1)} collective-permute-done((bf16[64,1024]{1,0:T(8,128)(2,1)S(1)}, bf16[64,1024]{1,0:T(8,128)(2,1)S(1)}, u32[]{:S(2)}, u32[]{:S(2)}) %collective-permute-start) | collective-permute-done | bytes 131104 | tf_op jit(solution)/shard_map/while/body/eval_jaxpr/ppermute | solution.py:15
  307.9 8.7 %conditional.4 = (f32[320,1024]{1,0:T(8,128)S(1)}, f32[320]{0:T(512)S(1)}) conditional(s32[]{:T(128)} %convert_element_type.282, () %tuple.78, (bf16[8,40,1024]{2,1,0:T(8,128)(2,1)S(1)}, bf16[2048,1024]{1,0:T(8,128)(2,1)}, bf16[8,40,1024]{2,1,0:T(8,128)(2,1)S(1)}, bf16[1024,2048]{1,0:T(8,128)(2,1)}) %tuple.79), branch_computations={%region_7.7_spmd, %region_8.9_spmd} | conditional | flops 4045537024 | bytes 61867336 | solution.py:124
  337.2 4.9 %all-to-all-done.3 = bf16[4,40,1024]{2,1,0:T(8,128)(2,1)S(1)} async-done(((bf16[4,40,1024]{2,1,0:T(8,128)(2,1)}), bf16[4,40,1024]{2,1,0:T(8,128)(2,1)S(1)}, u32[]{:S(2)}, u32[]{:S(2)}) %all-to-all-start.3) | async-done | bytes 327712 | tf_op jit(solution)/shard_map/while/body/eval_jaxpr/all_to_all | solution.py:178
  344.9 5.5 %collective-permute-done = bf16[64,1024]{1,0:T(8,128)(2,1)S(1)} collective-permute-done((bf16[64,1024]{1,0:T(8,128)(2,1)S(1)}, bf16[64,1024]{1,0:T(8,128)(2,1)S(1)}, u32[]{:S(2)}, u32[]{:S(2)}) %collective-permute-start) | collective-permute-done | bytes 131104 | tf_op jit(solution)/shard_map/while/body/eval_jaxpr/ppermute | solution.py:15
  376.4 8.7 %conditional.4 = (f32[320,1024]{1,0:T(8,128)S(1)}, f32[320]{0:T(512)S(1)}) conditional(s32[]{:T(128)} %convert_element_type.282, () %tuple.78, (bf16[8,40,1024]{2,1,0:T(8,128)(2,1)S(1)}, bf16[2048,1024]{1,0:T(8,128)(2,1)}, bf16[8,40,1024]{2,1,0:T(8,128)(2,1)S(1)}, bf16[1024,2048]{1,0:T(8,128)(2,1)}) %tuple.79), branch_computations={%region_7.7_spmd, %region_8.9_spmd} | conditional | flops 4045537024 | bytes 61867336 | solution.py:124
  405.6 4.9 %all-to-all-done.3 = bf16[4,40,1024]{2,1,0:T(8,128)(2,1)S(1)} async-done(((bf16[4,40,1024]{2,1,0:T(8,128)(2,1)}), bf16[4,40,1024]{2,1,0:T(8,128)(2,1)S(1)}, u32[]{:S(2)}, u32[]{:S(2)}) %all-to-all-start.3) | async-done | bytes 327712 | tf_op jit(solution)/shard_map/while/body/eval_jaxpr/all_to_all | solution.py:178
  413.4 5.5 %collective-permute-done = bf16[64,1024]{1,0:T(8,128)(2,1)S(1)} collective-permute-done((bf16[64,1024]{1,0:T(8,128)(2,1)S(1)}, bf16[64,1024]{1,0:T(8,128)(2,1)S(1)}, u32[]{:S(2)}, u32[]{:S(2)}) %collective-permute-start) | collective-permute-done | bytes 131104 | tf_op jit(solution)/shard_map/while/body/eval_jaxpr/ppermute | solution.py:15
  418.9 22.3 %all-reduce.1 = (bf16[1024]{0:T(1024)(128)(2,1)S(1)}, bf16[1024,4]{0,1:T(4,128)(2,1)S(1)}) all-reduce(bf16[1024]{0:T(1024)(128)(2,1)S(1)} %convert_element_type.153, bf16[1024,4]{0,1:T(4,128)(2,1)S(1)} %convert_element_type.155), channel_id=1, replica_groups=mesh['section'=4,'expert'=4,'dp'=2] {'expert','dp'}, use_global_device_ids=true, to_apply=%region_17.18 | all-reduce | flops 5120 | bytes 20480 | tf_op jit(solution)/shard_map/psum | solution.py:220
  (370 shorter events, 303.9 us)
Async XLA Ops:
  13.7 11.1 %all-to-all-start.1 = ((bf16[4,40,1024]{2,1,0:T(8,128)(2,1)}), bf16[4,40,1024]{2,1,0:T(8,128)(2,1)S(1)}, u32[]{:S(2)}, u32[]{:S(2)}) async-start(bf16[4,40,1024]{2,1,0:T(8,128)(2,1)} %bitcast.159), calls=%async_computation.1 | async-start | bytes 655360 | tf_op jit(solution)/shard_map/while/body/eval_jaxpr/all_to_all | solution.py:165
  24.7 9.0 %all-to-all-start = ((bf16[4,40,1024]{2,1,0:T(8,128)(2,1)}), bf16[4,40,1024]{2,1,0:T(8,128)(2,1)S(1)}, u32[]{:S(2)}, u32[]{:S(2)}) async-start(bf16[4,40,1024]{2,1,0:T(8,128)(2,1)} %bitcast.158), calls=%async_computation | async-start | bytes 655360 | tf_op jit(solution)/shard_map/while/body/eval_jaxpr/all_to_all | solution.py:166
  28.2 26.8 %reduce-scatter.2.cloned.1.call-start = ((), (), s32[]{:S(2)}) async-start(), calls=%async_computation.5 | async-start | bytes 1966080 | tf_op jit(solution)/shard_map/while/body/eval_jaxpr/reduce_scatter | solution.py:174
  56.8 10.3 %all-to-all-start.3 = ((bf16[4,40,1024]{2,1,0:T(8,128)(2,1)}), bf16[4,40,1024]{2,1,0:T(8,128)(2,1)S(1)}, u32[]{:S(2)}, u32[]{:S(2)}) async-start(bf16[4,40,1024]{2,1,0:T(8,128)(2,1)} %convert_element_type.283), calls=%async_computation.4 | async-start | bytes 655360 | tf_op jit(solution)/shard_map/while/body/eval_jaxpr/all_to_all | solution.py:178
  81.2 9.0 %all-to-all-start.1 = ((bf16[4,40,1024]{2,1,0:T(8,128)(2,1)}), bf16[4,40,1024]{2,1,0:T(8,128)(2,1)S(1)}, u32[]{:S(2)}, u32[]{:S(2)}) async-start(bf16[4,40,1024]{2,1,0:T(8,128)(2,1)} %bitcast.159), calls=%async_computation.1 | async-start | bytes 655360 | tf_op jit(solution)/shard_map/while/body/eval_jaxpr/all_to_all | solution.py:165
  90.2 9.0 %all-to-all-start = ((bf16[4,40,1024]{2,1,0:T(8,128)(2,1)}), bf16[4,40,1024]{2,1,0:T(8,128)(2,1)S(1)}, u32[]{:S(2)}, u32[]{:S(2)}) async-start(bf16[4,40,1024]{2,1,0:T(8,128)(2,1)} %bitcast.158), calls=%async_computation | async-start | bytes 655360 | tf_op jit(solution)/shard_map/while/body/eval_jaxpr/all_to_all | solution.py:166
  93.6 27.7 %reduce-scatter.2.cloned.1.call-start = ((), (), s32[]{:S(2)}) async-start(), calls=%async_computation.5 | async-start | bytes 1966080 | tf_op jit(solution)/shard_map/while/body/eval_jaxpr/reduce_scatter | solution.py:174
  123.2 10.3 %all-to-all-start.3 = ((bf16[4,40,1024]{2,1,0:T(8,128)(2,1)}), bf16[4,40,1024]{2,1,0:T(8,128)(2,1)S(1)}, u32[]{:S(2)}, u32[]{:S(2)}) async-start(bf16[4,40,1024]{2,1,0:T(8,128)(2,1)} %convert_element_type.283), calls=%async_computation.4 | async-start | bytes 655360 | tf_op jit(solution)/shard_map/while/body/eval_jaxpr/all_to_all | solution.py:178
  147.6 9.0 %all-to-all-start.1 = ((bf16[4,40,1024]{2,1,0:T(8,128)(2,1)}), bf16[4,40,1024]{2,1,0:T(8,128)(2,1)S(1)}, u32[]{:S(2)}, u32[]{:S(2)}) async-start(bf16[4,40,1024]{2,1,0:T(8,128)(2,1)} %bitcast.159), calls=%async_computation.1 | async-start | bytes 655360 | tf_op jit(solution)/shard_map/while/body/eval_jaxpr/all_to_all | solution.py:165
  156.5 9.0 %all-to-all-start = ((bf16[4,40,1024]{2,1,0:T(8,128)(2,1)}), bf16[4,40,1024]{2,1,0:T(8,128)(2,1)S(1)}, u32[]{:S(2)}, u32[]{:S(2)}) async-start(bf16[4,40,1024]{2,1,0:T(8,128)(2,1)} %bitcast.158), calls=%async_computation | async-start | bytes 655360 | tf_op jit(solution)/shard_map/while/body/eval_jaxpr/all_to_all | solution.py:166
  160.0 29.8 %reduce-scatter.2.cloned.1.call-start = ((), (), s32[]{:S(2)}) async-start(), calls=%async_computation.5 | async-start | bytes 1966080 | tf_op jit(solution)/shard_map/while/body/eval_jaxpr/reduce_scatter | solution.py:174
  191.7 10.3 %all-to-all-start.3 = ((bf16[4,40,1024]{2,1,0:T(8,128)(2,1)}), bf16[4,40,1024]{2,1,0:T(8,128)(2,1)S(1)}, u32[]{:S(2)}, u32[]{:S(2)}) async-start(bf16[4,40,1024]{2,1,0:T(8,128)(2,1)} %convert_element_type.283), calls=%async_computation.4 | async-start | bytes 655360 | tf_op jit(solution)/shard_map/while/body/eval_jaxpr/all_to_all | solution.py:178
  203.5 10.0 %collective-permute-start = (bf16[64,1024]{1,0:T(8,128)(2,1)S(1)}, bf16[64,1024]{1,0:T(8,128)(2,1)S(1)}, u32[]{:S(2)}, u32[]{:S(2)}) collective-permute-start(bf16[64,1024]{1,0:T(8,128)(2,1)S(1)} %get-tuple-element.681), channel_id=1, source_target_pairs={{8,0},{16,8},{24,16},{9,1},{17,9},{25,17},{10,2},{18,10},{26,18},{... | collective-permute-start | bytes 393224 | tf_op jit(solution)/shard_map/while/body/eval_jaxpr/ppermute | solution.py:15
  219.2 9.0 %all-to-all-start.1 = ((bf16[4,40,1024]{2,1,0:T(8,128)(2,1)}), bf16[4,40,1024]{2,1,0:T(8,128)(2,1)S(1)}, u32[]{:S(2)}, u32[]{:S(2)}) async-start(bf16[4,40,1024]{2,1,0:T(8,128)(2,1)} %bitcast.159), calls=%async_computation.1 | async-start | bytes 655360 | tf_op jit(solution)/shard_map/while/body/eval_jaxpr/all_to_all | solution.py:165
  228.2 9.0 %all-to-all-start = ((bf16[4,40,1024]{2,1,0:T(8,128)(2,1)}), bf16[4,40,1024]{2,1,0:T(8,128)(2,1)S(1)}, u32[]{:S(2)}, u32[]{:S(2)}) async-start(bf16[4,40,1024]{2,1,0:T(8,128)(2,1)} %bitcast.158), calls=%async_computation | async-start | bytes 655360 | tf_op jit(solution)/shard_map/while/body/eval_jaxpr/all_to_all | solution.py:166
  231.6 31.1 %reduce-scatter.2.cloned.1.call-start = ((), (), s32[]{:S(2)}) async-start(), calls=%async_computation.5 | async-start | bytes 1966080 | tf_op jit(solution)/shard_map/while/body/eval_jaxpr/reduce_scatter | solution.py:174
  264.6 9.0 %all-to-all-start.3 = ((bf16[4,40,1024]{2,1,0:T(8,128)(2,1)}), bf16[4,40,1024]{2,1,0:T(8,128)(2,1)S(1)}, u32[]{:S(2)}, u32[]{:S(2)}) async-start(bf16[4,40,1024]{2,1,0:T(8,128)(2,1)} %convert_element_type.283), calls=%async_computation.4 | async-start | bytes 655360 | tf_op jit(solution)/shard_map/while/body/eval_jaxpr/all_to_all | solution.py:178
  287.7 9.0 %all-to-all-start.1 = ((bf16[4,40,1024]{2,1,0:T(8,128)(2,1)}), bf16[4,40,1024]{2,1,0:T(8,128)(2,1)S(1)}, u32[]{:S(2)}, u32[]{:S(2)}) async-start(bf16[4,40,1024]{2,1,0:T(8,128)(2,1)} %bitcast.159), calls=%async_computation.1 | async-start | bytes 655360 | tf_op jit(solution)/shard_map/while/body/eval_jaxpr/all_to_all | solution.py:165
  296.7 9.0 %all-to-all-start = ((bf16[4,40,1024]{2,1,0:T(8,128)(2,1)}), bf16[4,40,1024]{2,1,0:T(8,128)(2,1)S(1)}, u32[]{:S(2)}, u32[]{:S(2)}) async-start(bf16[4,40,1024]{2,1,0:T(8,128)(2,1)} %bitcast.158), calls=%async_computation | async-start | bytes 655360 | tf_op jit(solution)/shard_map/while/body/eval_jaxpr/all_to_all | solution.py:166
  300.1 31.1 %reduce-scatter.2.cloned.1.call-start = ((), (), s32[]{:S(2)}) async-start(), calls=%async_computation.5 | async-start | bytes 1966080 | tf_op jit(solution)/shard_map/while/body/eval_jaxpr/reduce_scatter | solution.py:174
  333.1 9.0 %all-to-all-start.3 = ((bf16[4,40,1024]{2,1,0:T(8,128)(2,1)}), bf16[4,40,1024]{2,1,0:T(8,128)(2,1)S(1)}, u32[]{:S(2)}, u32[]{:S(2)}) async-start(bf16[4,40,1024]{2,1,0:T(8,128)(2,1)} %convert_element_type.283), calls=%async_computation.4 | async-start | bytes 655360 | tf_op jit(solution)/shard_map/while/body/eval_jaxpr/all_to_all | solution.py:178
  365.1 9.0 %all-to-all-start = ((bf16[4,40,1024]{2,1,0:T(8,128)(2,1)}), bf16[4,40,1024]{2,1,0:T(8,128)(2,1)S(1)}, u32[]{:S(2)}, u32[]{:S(2)}) async-start(bf16[4,40,1024]{2,1,0:T(8,128)(2,1)} %bitcast.158), calls=%async_computation | async-start | bytes 655360 | tf_op jit(solution)/shard_map/while/body/eval_jaxpr/all_to_all | solution.py:166
  368.6 31.1 %reduce-scatter.2.cloned.1.call-start = ((), (), s32[]{:S(2)}) async-start(), calls=%async_computation.5 | async-start | bytes 1966080 | tf_op jit(solution)/shard_map/while/body/eval_jaxpr/reduce_scatter | solution.py:174
  401.5 9.0 %all-to-all-start.3 = ((bf16[4,40,1024]{2,1,0:T(8,128)(2,1)}), bf16[4,40,1024]{2,1,0:T(8,128)(2,1)S(1)}, u32[]{:S(2)}, u32[]{:S(2)}) async-start(bf16[4,40,1024]{2,1,0:T(8,128)(2,1)} %convert_element_type.283), calls=%async_computation.4 | async-start | bytes 655360 | tf_op jit(solution)/shard_map/while/body/eval_jaxpr/all_to_all | solution.py:178
  (49 other events, 294.1 us)
Sparse Core Ops, SparseCore 0:
  37.3 17.5 reduce-scatter.1
  102.8 18.5 reduce-scatter.1
  169.2 20.5 reduce-scatter.1
  249.4 8.8 reduce-scatter.1
  317.8 7.4 reduce-scatter.1
  386.3 5.9 reduce-scatter.1
where the time goes:
time: 453 us; the launch traced here: 449 us
  waiting for transfers between devices  153 us (34%)
  starting transfers between devices  92.7 us (20%)
  blocking collectives  64.3 us (14%)
  matrix products  56.8 us (13%)
  other arithmetic  42.8 us (9%)
  local copies, waits for them, and re-layouts  19.9 us (4%)
  between operations  14.1 us (3%)
  loops' own time  5.49 us (1%)
    ppermute x6, waiting for transfers between devices, from_behind(): return lax.ppermute(shard, axis, pairs)  36.5 us
    all_to_all x6, waiting for transfers between devices, step_fn(): lax.all_to_all(summed_u.astype(jnp.bfloat16), 'expert', split_axis=0, con...  31.8 us
    all_to_all x6, waiting for transfers between devices, step_fn(): lax.all_to_all(summed_g.astype(jnp.bfloat16), 'expert', split_axis=0, con...  27.2 us
    all_to_all x6, starting transfers between devices, step_fn(): lax.all_to_all(sent_u, 'expert', split_axis=0, concat_axis=0, tiled=True)  22.4 us
    psum x1, blocking collectives, per_device(): lax.psum(final_state[2].astype(jnp.bfloat16), ('expert', 'dp'))  22.3 us
    all_to_all x6, starting transfers between devices, step_fn(): lax.all_to_all(summed_u.astype(jnp.bfloat16), 'expert', split_axis=0, con...  22.2 us
    all_to_all x6, waiting for transfers between devices, step_fn(): lax.all_to_all(sent_u, 'expert', split_axis=0, concat_axis=0, tiled=True)  21.9 us
    all_to_all x6, starting transfers between devices, step_fn(): lax.all_to_all(sent_grad, 'expert', split_axis=0, concat_axis=0, tiled=True)  20.7 us
  transfers between devices with their start and end apart: 36, of which 33 were waited for; matrix products, arithmetic and copies ran while one was open for 7% of the time, Pallas kernels for 0%

commit v1 on v0

v1 whole, which is shorter than its diff:
```python
import functools
import math

import jax
import jax.numpy as jnp
from jax import lax
from jax.experimental import pallas as pl
from jax.experimental.pallas import tpu as pltpu
from jax.sharding import PartitionSpec as P

GELU_C = math.sqrt(2.0 / math.pi)
LANES = 128
VMEM_BYTES = 40 * 1024 * 1024
F32 = jnp.float32
BF16 = jnp.bfloat16
NT = (((1,), (1,)), ((), ()))
TN = (((0,), (0,)), ((), ()))


def peers(count):
    if count & (count - 1) == 0:
        return [[(i, i ^ j) for i in range(count)] for j in range(1, count)]
    return [[(i, (i + j) % count) for i in range(count)] for j in range(1, count)]


def relative(ids, me, count):
    if count & (count - 1) == 0:
        return jnp.bitwise_xor(ids, me)
    return jnp.remainder(ids - me + count, count)


def exchange(chunks, back=False):
    count = len(chunks)
    out = [chunks[0]]
    for j, pairs in enumerate(peers(count), 1):
        moved = [(b, a) for a, b in pairs] if back else pairs
        out.append(lax.ppermute(chunks[j], "expert", moved))
    return out


def split_hi_lo(values):
    hi = values.astype(BF16)
    return hi, (values - hi.astype(F32)).astype(BF16)


def hidden_kernel(pick_ref, u_ref, *refs, halves, steps, width):
    first_refs, (active_ref, slope_ref) = refs[:halves], refs[halves:]
    step = pl.program_id(0)
    for half in range(halves):

        @pl.when(step // steps == half)
        def _(half=half):
            hidden = jnp.dot(
                u_ref[0, :, :width], first_refs[half][...], preferred_element_type=F32
            )
            square = hidden * hidden
            tanh_val = jnp.tanh(GELU_C * hidden * (1.0 + 0.044715 * square))
            up = 0.5 * (1.0 + tanh_val)
            active_ref[...] = (hidden * up).astype(BF16)
            rise = (GELU_C * hidden) * (1.0 + 3.0 * 0.044715 * square)
            slope_ref[...] = (up * (1.0 + (1.0 - tanh_val) * rise)).astype(BF16)


def half_spec(shape, axis, half, steps):
    def place(i, *_):
        at = jnp.clip(i - half * steps, 0, steps - 1)
        return (at, 0) if axis == 0 else (0, at)

    return pl.BlockSpec(shape, place)


def run_hidden(pick, stack, first_parts, tile):
    rows, packed = stack.shape[1], stack.shape[2]
    width, part = first_parts[0].shape
    halves, steps = len(first_parts), part // tile
    out = jax.ShapeDtypeStruct((rows, halves * part), BF16)
    return pl.pallas_call(
        functools.partial(hidden_kernel, halves=halves, steps=steps, width=width),
        grid_spec=pltpu.PrefetchScalarGridSpec(
            num_scalar_prefetch=1,
            grid=(halves * steps,),
            in_specs=[pl.BlockSpec((1, rows, packed), lambda i, pick: (pick[0], 0, 0))]
            + [half_spec((width, tile), 1, half, steps) for half in range(halves)],
            out_specs=[pl.BlockSpec((rows, tile), lambda i, pick: (0, i))] * 2,
        ),
        out_shape=[out, out],
        compiler_params=pltpu.CompilerParams(vmem_limit_bytes=VMEM_BYTES),
        cost_estimate=pl.CostEstimate(
            flops=2 * rows * width * halves * part,
            bytes_accessed=2 * width * halves * part,
            transcendentals=rows * halves * part,
        ),
        name="hidden",
    )(pick, stack, *first_parts)


def expert_kernel(pick_ref, u_ref, grad_ref, active_ref, slope_ref, *refs, halves, steps, width, experts):
    first_refs, second_refs = refs[:halves], refs[halves : 2 * halves]
    router_ref, gain_ref, sums_in_ref, out_ref, sums_ref, slot_acc, gate_acc = refs[2 * halves :]
    step = pl.program_id(0)

    @pl.when(step == 0)
    def _():
        slot_acc[...] = jnp.zeros_like(slot_acc)
        gate_acc[...] = jnp.zeros_like(gate_acc)

    for half in range(halves):

        @pl.when(step // steps == half)
        def _(half=half):
            back = lax.dot_general(
                grad_ref[...], second_refs[half][...], NT, preferred_element_type=F32
            )
            product = active_ref[...].astype(F32) * back
            folded = product[:, :LANES]
            for at in range(LANES, product.shape[1], LANES):
                folded = folded + product[:, at : at + LANES]
            gate_acc[...] += folded
            pre = (back * slope_ref[...].astype(F32)).astype(BF16)
            slot_acc[...] += lax.dot_general(
                pre, first_refs[half][...], NT, preferred_element_type=F32
            )

    @pl.when(step == halves * steps - 1)
    def _():
        meta = u_ref[0, :, width:].astype(F32)
        unit_gain = u_ref[0, :, :width]
        gate = meta[:, experts : experts + 1] + meta[:, experts + 1 : experts + 2]
        both = meta[:, experts + 2 : experts + 3] + meta[:, experts + 3 : experts + 4]
        dots = jnp.sum(gate_acc[...], axis=1, keepdims=True)
        lane = lax.broadcasted_iota(jnp.int32, meta.shape, 1)
        dlogits = jnp.where(lane < experts, meta, 0.0) * (both * dots)
        high, low = split_hi_lo(dlogits)
        router_rows = jnp.dot(high, router_ref[...], preferred_element_type=F32) + jnp.dot(
            low, router_ref[...], preferred_element_type=F32
        )
        result = gate * slot_acc[...] + router_rows
        out_ref[...] = result.astype(BF16)
        gain_part = jnp.sum(result * unit_gain.astype(F32), axis=0, keepdims=True) / gain_ref[...]
        router_part = lax.dot_general(high, unit_gain, TN, preferred_element_type=F32)
        sums_ref[:8, :] = sums_in_ref[:8, :] + jnp.broadcast_to(gain_part, (8, width))
        sums_ref[8:, :] = sums_in_ref[8:, :] + router_part[: sums_ref.shape[0] - 8, :]


def run_experts(pick, stack, grad_rows, active, slope, first_parts, second_parts, router_pad, gain, sums, experts, tile):
    rows, packed = stack.shape[1], stack.shape[2]
    width, part = first_parts[0].shape
    halves, steps = len(first_parts), part // tile

    def whole(shape):
        return pl.BlockSpec(shape, lambda i, pick: (0,) * len(shape))

    return pl.pallas_call(
        functools.partial(expert_kernel, halves=halves, steps=steps, width=width, experts=experts),
        grid_spec=pltpu.PrefetchScalarGridSpec(
            num_scalar_prefetch=1,
            grid=(halves * steps,),
            in_specs=[
                pl.BlockSpec((1, rows, packed), lambda i, pick: (pick[0], 0, 0)),
                whole((rows, width)),
                pl.BlockSpec((rows, tile), lambda i, pick: (0, i)),
                pl.BlockSpec((rows, tile), lambda i, pick: (0, i)),
            ]
            + [half_spec((width, tile), 1, half, steps) for half in range(halves)]
            + [half_spec((tile, width), 0, half, steps) for half in range(halves)]
            + [whole(router_pad.shape), whole(gain.shape), whole(sums.shape)],
            out_specs=[whole((rows, width)), whole(sums.shape)],
            scratch_shapes=[pltpu.VMEM((rows, width), F32), pltpu.VMEM((rows, LANES), F32)],
        ),
        out_shape=[
            jax.ShapeDtypeStruct((rows, width), BF16),
            jax.ShapeDtypeStruct(sums.shape, F32),
        ],
        compiler_params=pltpu.CompilerParams(vmem_limit_bytes=VMEM_BYTES),
        cost_estimate=pl.CostEstimate(
            flops=4 * rows * width * halves * part,
            bytes_accessed=4 * width * halves * part,
            transcendentals=0,
        ),
        name="expert",
    )(pick, stack, grad_rows, active, slope, *first_parts, *second_parts, router_pad, gain, sums)


def token_kernel(pick_ref, acts_ref, gain_ref, target_ref, ret_ref, grad_ref, out_ref):
    pick = pick_ref[0]
    values = acts_ref[pick].astype(F32)
    centred = values - jnp.mean(values, axis=-1, keepdims=True)
    inverse = lax.rsqrt(jnp.mean(centred * centred, axis=-1, keepdims=True) + 1e-06)
    unit = centred * inverse
    target = target_ref[pick]
    place = lax.broadcasted_iota(jnp.int32, (values.shape[0], ret_ref.shape[0]), 1)
    hit = jnp.logical_or(place == target[:, 0:1], place == target[:, 1:2])
    norm_grad = jnp.dot(
        jnp.where(hit, 1.0, 0.0).astype(BF16), ret_ref[...], preferred_element_type=F32
    )
    scaled = norm_grad * gain_ref[...]
    change = inverse * (
        scaled
        - jnp.mean(scaled, axis=-1, keepdims=True)
        - unit * jnp.mean(scaled * unit, axis=-1, keepdims=True)
    )
    out_ref[...] = (grad_ref[...].astype(F32) + change).astype(BF16)


def run_tokens(pick, acts, gain, target, ret, grad):
    smem = pl.BlockSpec(memory_space=pltpu.SMEM)
    vmem = pl.BlockSpec(memory_space=pltpu.VMEM)
    return pl.pallas_call(
        token_kernel,
        in_specs=[smem] + [vmem] * 5,
        out_specs=vmem,
        out_shape=jax.ShapeDtypeStruct(grad.shape, BF16),
        name="token",
    )(pick, acts, gain, target, ret, grad)


def rows_kernel(pick_ref, target_ref, in_ref, last_ref, grad_ref, rows_ref):
    pick = pick_ref[0]
    grad = jnp.where(pick_ref[1] > 0, last_ref[pick], in_ref[...])
    grad_ref[...] = grad
    target = target_ref[pick]
    place = lax.broadcasted_iota(jnp.int32, (rows_ref.shape[0], grad.shape[0]), 0)
    hit = jnp.logical_or(place == target[0:1, :], place == target[1:2, :])
    rows_ref[...] = jnp.dot(
        jnp.where(hit, 1.0, 0.0).astype(BF16), grad, preferred_element_type=F32
    ).astype(BF16)


def run_rows(pick, target_t, incoming, last_grad, slots):
    smem = pl.BlockSpec(memory_space=pltpu.SMEM)
    vmem = pl.BlockSpec(memory_space=pltpu.VMEM)
    return pl.pallas_call(
        rows_kernel,
        in_specs=[smem] + [vmem] * 3,
        out_specs=[vmem] * 2,
        out_shape=[
            jax.ShapeDtypeStruct(incoming.shape, BF16),
            jax.ShapeDtypeStruct((slots, incoming.shape[1]), BF16),
        ],
        name="rows",
    )(pick, target_t, incoming, last_grad)


def per_device(acts, out_grad, ln_gain, router, w_in, w_out, expert_ids, slot_ids, capacity):
    sections = lax.axis_size("section")
    section = lax.axis_index("section")
    me = lax.axis_index("expert")
    cores = lax.axis_size("dp")
    micro = acts.shape[1]
    tokens = acts.shape[2]
    width = acts.shape[3]
    experts = router.shape[2]
    top = expert_ids.shape[3]
    cap = 5 * tokens * top // (4 * experts)
    slots = experts * cap
    all_tokens = tokens * lax.axis_size("expert") * cores
    scale = 1.0 / math.sqrt(micro * all_tokens)
    tile = 512
    acts, ids, places, caps = acts[0], expert_ids[0], slot_ids[0], capacity[0]
    router_w = router[0]

    first_parts, second_parts = [w_in[0, 0]], [w_out[0, 0]]
    for by in range(1, cores):
        turn = [(i, (i + by) % cores) for i in range(cores)]
        first_parts.append(lax.ppermute(w_in[0, 0], "dp", turn))
    for by in range(1, cores):
        turn = [(i, (i + by) % cores) for i in range(cores)]
        second_parts.append(lax.ppermute(w_out[0, 0], "dp", turn))

    columns = jnp.arange(experts, dtype=jnp.int32)
    router_pad = jnp.zeros((LANES, width), BF16).at[:experts].set(router_w.T)
    pick_bool = ids[..., None] == columns
    table = pick_bool.astype(F32)
    kept = places < jnp.sum(jnp.where(pick_bool, caps[:, None, None, :], 0), axis=-1)
    target = jnp.where(kept, relative(ids, me, experts) * cap + places, -1)
    target_t = jnp.swapaxes(target, 1, 2)
    positions = jnp.arange(slots, dtype=jnp.int32)

    def forward_rows(m, grad):
        values = acts[m].astype(F32)
        centred = values - jnp.mean(values, axis=-1, keepdims=True)
        inverse = lax.rsqrt(jnp.mean(centred * centred, axis=-1, keepdims=True) + 1e-06)
        normed = (centred * inverse * ln_gain[0]).astype(BF16)
        logits = jnp.dot(normed, router_w, preferred_element_type=F32)
        chosen = jnp.sum(table[m] * logits[:, None, :], axis=2)
        gate1 = 1.0 / (1.0 + jnp.exp(chosen[:, 1] - chosen[:, 0]))
        gates = jnp.stack([gate1, 1.0 - gate1], axis=1)
        both = jnp.broadcast_to((gates[:, 0] * gates[:, 1])[:, None], gates.shape)
        meta = [table[m] - table[m][:, ::-1]]
        for values in split_hi_lo(gates) + split_hi_lo(both):
            meta.append(values[:, :, None].astype(F32))
        meta = jnp.concatenate(meta, axis=2)
        meta = jnp.pad(meta, ((0, 0), (0, 0), (0, LANES - meta.shape[2]))).astype(BF16)
        hit = (positions[:, None, None] == target[m][None]).astype(BF16)
        send = hit[:, :, 0] + hit[:, :, 1]
        sent = [jnp.dot(send, normed, preferred_element_type=F32).astype(BF16)]
        sent.append(
            jnp.einsum("ptk,tkc->pc", hit, meta, preferred_element_type=F32).astype(BF16)
        )
        if grad is not None:
            sent.append(jnp.dot(send, grad, preferred_element_type=F32).astype(BF16))
        return jnp.concatenate(sent, axis=1)

    def chunks_of(rows):
        return [rows[j * cap : (j + 1) * cap] for j in range(experts)]

    def picked(step):
        number = step - (sections - 1 - section)
        is_last = jnp.logical_and(section == sections - 1, step < micro)
        return jnp.stack([jnp.clip(number, 0, micro - 1), is_last.astype(jnp.int32)]).astype(jnp.int32)

    on_last = section == sections - 1
    grad0 = jnp.where(on_last, out_grad[0], jnp.zeros_like(out_grad[0]))
    packed0 = jnp.concatenate(exchange(chunks_of(forward_rows(0, grad0))), axis=0)
    split = width + LANES
    u0, grad_rows = packed0[None, :, :split], packed0[:, split:]
    rest = [forward_rows(m, None) for m in range(1, micro)]
    rest = exchange(
        [jnp.stack([rows[j * cap : (j + 1) * cap] for rows in rest]) for j in range(experts)]
    )
    stack = jnp.concatenate([u0, jnp.concatenate(rest, axis=1)], axis=0)

    sums = jnp.zeros((8 + -(-experts // 8) * 8, width), F32)
    gain = ln_gain
    grad = grad0
    steps = micro + sections - 1
    results = []
    down = [(i, i - 1) for i in range(1, sections)]
    for step in range(steps):
        pick = picked(step)
        rows_u = u0 if step == 0 else stack
        if step > 0:
            incoming = lax.ppermute(results[-1], "section", down)
            grad, sent = run_rows(pick, target_t, incoming, out_grad, slots)
            grad_rows = jnp.concatenate(exchange(chunks_of(sent)), axis=0)
        active, slope = run_hidden(pick, rows_u, first_parts, tile)
        slot_rows, sums = run_experts(
            pick, rows_u, grad_rows, active, slope, first_parts, second_parts,
            router_pad, gain, sums, experts, tile,
        )
        chunks = chunks_of(slot_rows)
        if step == steps - 1:
            tail = jnp.concatenate([sums[:1], sums[8 : 8 + experts]], axis=0).astype(BF16)
            tail = jnp.pad(tail, ((0, -(cap + 1 + experts) % 16), (0, 0)))
            chunks = [jnp.concatenate([chunk, tail], axis=0) for chunk in chunks]
        back = exchange(chunks, back=True)
        ret = jnp.concatenate([chunk[:cap] for chunk in back], axis=0)
        results.append(run_tokens(pick, acts, gain, target, ret, grad))

    total = sum(chunk[cap : cap + 1 + experts].astype(F32) for chunk in back)
    shared = total
    for by in range(1, cores):
        shared = shared + lax.ppermute(total, "dp", [(i, (i + by) % cores) for i in range(cores)])
    shared = shared * scale
    every = jnp.stack(results)
    grads = lax.dynamic_slice_in_dim(every, sections - 1 - section, micro, axis=0)
    return (grads[None], shared[:1], shared[1:].T[None])


def solution(mesh):
    return jax.shard_map(
        per_device,
        mesh=mesh,
        in_specs=(
            P("section", None, ("expert", "dp"), None),
            P(None, ("expert", "dp"), None),
            P("section", None),
            P("section", None, None),
            P("section", "expert", None, "dp"),
            P("section", "expert", "dp", None),
            P("section", None, ("expert", "dp"), None),
            P("section", None, ("expert", "dp"), None),
            P("section", None, None),
        ),
        out_specs=(
            P("section", None, ("expert", "dp"), None),
            P("section", None),
            P("section", None, None),
        ),
        check_vma=False,
    )
```

time: 453 us -> 305 us (0.67)
  Pallas kernels: 0 us -> 144 us
  waiting for transfers between devices: 153 us -> 51.1 us
  blocking collectives: 64.3 us -> 0 us
  matrix products: 56.8 us -> 2.72 us
  starting transfers between devices: 92.7 us -> 56.5 us
  other arithmetic: 42.8 us -> 9.84 us
  local copies, waits for them, and re-layouts: 19.9 us -> 37.1 us
  between operations: 14.1 us -> 1.91 us
  loops' own time: 5.49 us -> 0 us
    pallas_call x0 -> x22, Pallas kernels: none -> 144 us  [the longest x6 76 us: run_experts(): pl.pallas_call(functools.partial(expert_kernel, halves=halves, steps=step...]
    all_to_all x24 -> x0, waiting for transfers between devices: 99.9 us -> none  [the longest x6 31.8 us: step_fn(): lax.all_to_all(summed_u.astype(jnp.bfloat16), 'expert', split_axis=0, con...]
    all_to_all x24 -> x0, starting transfers between devices: 84.7 us -> none  [the longest x6 22.4 us: step_fn(): lax.all_to_all(sent_u, 'expert', split_axis=0, concat_axis=0, tiled=True)]
    dot_general x45 -> x10, matrix products: 56.8 us -> 2.72 us  [the longest x3 0.92 us: forward_rows(): sent = [jnp.dot(send, normed, preferred_element_type=F32).astype(BF16)]]
    ppermute x6 -> x47, starting transfers between devices: 7.75 us -> 56.5 us  [the longest x39 49 us: exchange(): out.append(lax.ppermute(chunks[j], 'expert', moved))]
    all_gather x12 -> x0, blocking collectives: 27.2 us -> none  [the longest x6 13.7 us: step_fn(): lax.all_gather(recv_u, 'dp', axis=0, tiled=True)]
    unnamed x3 -> x104, local copies, waits for them, and re-layouts: 0.69 us -> 24.2 us
    psum x1 -> x0, blocking collectives: 22.3 us -> none  [per_device(): lax.psum(final_state[2].astype(jnp.bfloat16), ('expert', 'dp'))]
  transfers between devices with their start and end apart: 36 -> 47, of which waited for: 33 -> 27; matrix products, arithmetic and copies ran while one was open for 7% -> 4% of each run, Pallas kernels for 0% -> 20%
where the time goes in v1:
time: 305 us; the launch traced here: 303 us
  Pallas kernels  144 us (47%)
  starting transfers between devices  56.5 us (19%)
  waiting for transfers between devices  51.1 us (17%)
  local copies, waits for them, and re-layouts  37.1 us (12%)
  other arithmetic  9.84 us (3%)
    pallas_call x6, Pallas kernels, run_experts(): pl.pallas_call(functools.partial(expert_kernel, halves=halves, steps=step...  76 us
    ppermute x39, starting transfers between devices, exchange(): out.append(lax.ppermute(chunks[j], 'expert', moved))  49 us
    pallas_call x6, Pallas kernels, run_hidden(): pl.pallas_call(functools.partial(hidden_kernel, halves=halves, steps=step...  46.6 us
    ppermute x39, waiting for transfers between devices, exchange(): out.append(lax.ppermute(chunks[j], 'expert', moved))  29.9 us
    unnamed x104, local copies, waits for them, and re-layouts  24.2 us
    ppermute x5, waiting for transfers between devices, per_device(): incoming = lax.ppermute(results[-1], 'section', down)  21.1 us
    pallas_call x5, Pallas kernels, run_tokens(): pl.pallas_call(token_kernel, in_specs=[smem] + [vmem] * 5, out_specs=vmem...  11.1 us
    pallas_call x5, Pallas kernels, run_rows(): pl.pallas_call(rows_kernel, in_specs=[smem] + [vmem] * 3, out_specs=[vmem...  10.2 us
  transfers between devices with their start and end apart: 47, of which 27 were waited for; matrix products, arithmetic and copies ran while one was open for 4% of the time, Pallas kernels for 20%

profile of v1, /device:TPU:0, one launch (start us, length us, event | category | flops | bytes accessed | tf_op | source)
XLA Modules:
  0.0 303.1 jit_solution(1785984257039904982)
XLA Ops:
  7.6 4.0 %collective-permute-start.2 = (bf16[40,2176]{1,0:T(8,128)(2,1)S(1)}, bf16[40,2176]{1,0:T(8,128)(2,1)S(1)}, u32[]{:S(2)}, u32[]{:S(2)}) collective-permute-start(bf16[40,2176]{1,0:T(8,128)(2,1)S(1)} %get-tuple-element.99), channel_id=1, source_target_pairs={{0,6},{2,4},{4,2},{6,0},{1,7},{3,5},{5,3},{7,1},{8,14},{10,12},{12... | collective-permute-start | bytes 522248 | tf_op jit(solution)/shard_map/ppermute | solution.py:37
  16.8 3.0 collective-permute-start.10
  21.7 7.8 %hidden.6 = (bf16[160,4096]{1,0:T(8,128)(2,1)S(1)}, bf16[160,4096]{1,0:T(8,128)(2,1)S(1)}) custom-call(s32[2]{0:T(128)S(1)} %pad_add_fusion.3.pick_ref, bf16[1,160,1152]{2,1,0:T(8,128)(2,1)S(1)} %slice_bitcast_fusion.u_ref, bf16[1024,2048]{1,0:T(8,128)(2,1)S(1)} %bitcast.191, bf16[1024,2048]{1,0:T(8,128)(2,1)} %collective-permute-done.3.refs_1_), custom_call_target="tpu_custom_call" | custom-call | flops 1342177280 | bytes 8388608 | tf_op jit(solution)/shard_map/hidden/pallas_call | solution.py:77
  29.5 12.7 %expert.6 = (bf16[160,1024]{1,0:T(8,128)(2,1)S(1)}, f32[16,1024]{1,0:T(8,128)S(1)}) custom-call(s32[2]{0:T(128)S(1)} %pad_add_fusion.3.pick_ref, bf16[1,160,1152]{2,1,0:T(8,128)(2,1)S(1)} %slice_bitcast_fusion.u_ref, bf16[160,1024]{1,0:T(8,128)(2,1)S(1)} %pad_maximum_fusion.2.grad_ref, bf16[160,4096]{1,0:T(8,128)(2,1)S(1)} %get-tuple-element.49.active_ref, ...), custom_call_target="tpu_custom_call" | custom-call | flops 2684354560 | bytes 16777216 | tf_op jit(solution)/shard_map/expert/pallas_call | solution.py:153
  49.6 3.3 %collective-permute-done.5 = bf16[40,1024]{1,0:T(8,128)(2,1)S(1)} collective-permute-done((bf16[40,1024]{1,0:T(8,128)(2,1)S(1)}, bf16[40,1024]{1,0:T(8,128)(2,1)S(1)}, u32[]{:S(2)}, u32[]{:S(2)}) %collective-permute-start.5) | collective-permute-done | bytes 81952 | tf_op jit(solution)/shard_map/ppermute | solution.py:37
  57.4 5.6 %collective-permute-done.11.in_ref = bf16[64,1024]{1,0:T(8,128)(2,1)S(1)} collective-permute-done((bf16[64,1024]{1,0:T(8,128)(2,1)}, bf16[64,1024]{1,0:T(8,128)(2,1)S(1)}, u32[]{:S(2)}, u32[]{:S(2)}) %collective-permute-start.11) | collective-permute-done | bytes 131104 | tf_op jit(solution)/shard_map/ppermute | solution.py:333
  72.5 7.8 %hidden.7 = (bf16[160,4096]{1,0:T(8,128)(2,1)S(1)}, bf16[160,4096]{1,0:T(8,128)(2,1)S(1)}) custom-call(s32[2]{0:T(128)S(1)} %copy-done.23, bf16[3,160,1152]{2,1,0:T(8,128)(2,1)S(1)} %maximum_maximum_fusion.u_ref, bf16[1024,2048]{1,0:T(8,128)(2,1)S(1)} %bitcast.193, bf16[1024,2048]{1,0:T(8,128)(2,1)} %collective-permute-done.3.refs_1_), custom_call_target="tpu_custom_call" | custom-call | flops 1342177280 | bytes 8388608 | tf_op jit(solution)/shard_map/hidden/pallas_call | solution.py:77
  80.3 12.7 %expert.7 = (bf16[160,1024]{1,0:T(8,128)(2,1)S(1)}, f32[16,1024]{1,0:T(8,128)S(1)}) custom-call(s32[2]{0:T(128)S(1)} %copy-done.23, bf16[3,160,1152]{2,1,0:T(8,128)(2,1)S(1)} %maximum_maximum_fusion.u_ref, bf16[160,1024]{1,0:T(8,128)(2,1)S(1)} %pad_maximum_fusion.4.grad_ref, bf16[160,4096]{1,0:T(8,128)(2,1)S(1)} %get-tuple-element.53.active_ref, ...), custom_call_target="tpu_custom_call" | custom-call | flops 2684354560 | bytes 16777216 | tf_op jit(solution)/shard_map/expert/pallas_call | solution.py:153
  100.3 2.2 token_.7
  104.6 4.9 %collective-permute-done.18.in_ref = bf16[64,1024]{1,0:T(8,128)(2,1)S(1)} collective-permute-done((bf16[64,1024]{1,0:T(8,128)(2,1)}, bf16[64,1024]{1,0:T(8,128)(2,1)S(1)}, u32[]{:S(2)}, u32[]{:S(2)}) %collective-permute-start.18) | collective-permute-done | bytes 131104 | tf_op jit(solution)/shard_map/ppermute | solution.py:333
  119.7 7.8 %hidden.8 = (bf16[160,4096]{1,0:T(8,128)(2,1)S(1)}, bf16[160,4096]{1,0:T(8,128)(2,1)S(1)}) custom-call(s32[2]{0:T(128)S(1)} %copy-done.25, bf16[3,160,1152]{2,1,0:T(8,128)(2,1)S(1)} %maximum_maximum_fusion.u_ref, bf16[1024,2048]{1,0:T(8,128)(2,1)S(1)} %bitcast.195, bf16[1024,2048]{1,0:T(8,128)(2,1)} %collective-permute-done.3.refs_1_), custom_call_target="tpu_custom_call" | custom-call | flops 1342177280 | bytes 8388608 | tf_op jit(solution)/shard_map/hidden/pallas_call | solution.py:77
  127.6 12.7 %expert.8 = (bf16[160,1024]{1,0:T(8,128)(2,1)S(1)}, f32[16,1024]{1,0:T(8,128)S(1)}) custom-call(s32[2]{0:T(128)S(1)} %copy-done.26, bf16[3,160,1152]{2,1,0:T(8,128)(2,1)S(1)} %maximum_maximum_fusion.u_ref, bf16[160,1024]{1,0:T(8,128)(2,1)S(1)} %pad_maximum_fusion.6.grad_ref, bf16[160,4096]{1,0:T(8,128)(2,1)S(1)} %get-tuple-element.59.active_ref, ...), custom_call_target="tpu_custom_call" | custom-call | flops 2684354560 | bytes 16777216 | tf_op jit(solution)/shard_map/expert/pallas_call | solution.py:153
  148.5 2.2 token_.8
  152.7 5.1 %collective-permute-done.25.in_ref = bf16[64,1024]{1,0:T(8,128)(2,1)S(1)} collective-permute-done((bf16[64,1024]{1,0:T(8,128)(2,1)}, bf16[64,1024]{1,0:T(8,128)(2,1)S(1)}, u32[]{:S(2)}, u32[]{:S(2)}) %collective-permute-start.25) | collective-permute-done | bytes 131104 | tf_op jit(solution)/shard_map/ppermute | solution.py:333
  167.9 7.8 %hidden.9 = (bf16[160,4096]{1,0:T(8,128)(2,1)S(1)}, bf16[160,4096]{1,0:T(8,128)(2,1)S(1)}) custom-call(s32[2]{0:T(128)S(1)} %copy-done.24, bf16[3,160,1152]{2,1,0:T(8,128)(2,1)S(1)} %maximum_maximum_fusion.u_ref, bf16[1024,2048]{1,0:T(8,128)(2,1)S(1)} %bitcast.197, bf16[1024,2048]{1,0:T(8,128)(2,1)} %collective-permute-done.3.refs_1_), custom_call_target="tpu_custom_call" | custom-call | flops 1342177280 | bytes 8388608 | tf_op jit(solution)/shard_map/hidden/pallas_call | solution.py:77
  175.7 12.7 %expert.9 = (bf16[160,1024]{1,0:T(8,128)(2,1)S(1)}, f32[16,1024]{1,0:T(8,128)S(1)}) custom-call(s32[2]{0:T(128)S(1)} %copy-done.24, bf16[3,160,1152]{2,1,0:T(8,128)(2,1)S(1)} %maximum_maximum_fusion.u_ref, bf16[160,1024]{1,0:T(8,128)(2,1)S(1)} %pad_maximum_fusion.8.grad_ref, bf16[160,4096]{1,0:T(8,128)(2,1)S(1)} %get-tuple-element.65.active_ref, ...), custom_call_target="tpu_custom_call" | custom-call | flops 2684354560 | bytes 16777216 | tf_op jit(solution)/shard_map/expert/pallas_call | solution.py:153
  195.7 2.2 token_.9
  201.4 7.8 %hidden.10 = (bf16[160,4096]{1,0:T(8,128)(2,1)S(1)}, bf16[160,4096]{1,0:T(8,128)(2,1)S(1)}) custom-call(s32[2]{0:T(128)S(1)} %pad_add_fusion.1.pick_ref, bf16[3,160,1152]{2,1,0:T(8,128)(2,1)S(1)} %maximum_maximum_fusion.u_ref, bf16[1024,2048]{1,0:T(8,128)(2,1)S(1)} %bitcast.199, bf16[1024,2048]{1,0:T(8,128)(2,1)} %collective-permute-done.3.refs_1_), custom_call_target="tpu_custom_call" | custom-call | flops 1342177280 | bytes 8388608 | tf_op jit(solution)/shard_map/hidden/pallas_call | solution.py:77
  210.2 7.8 %hidden.11 = (bf16[160,4096]{1,0:T(8,128)(2,1)S(1)}, bf16[160,4096]{1,0:T(8,128)(2,1)S(1)}) custom-call(s32[2]{0:T(128)S(1)} %pad_add_fusion.pick_ref, bf16[3,160,1152]{2,1,0:T(8,128)(2,1)S(1)} %maximum_maximum_fusion.u_ref, bf16[1024,2048]{1,0:T(8,128)(2,1)S(1)} %bitcast.200, bf16[1024,2048]{1,0:T(8,128)(2,1)} %collective-permute-done.3.refs_1_), custom_call_target="tpu_custom_call" | custom-call | flops 1342177280 | bytes 8388608 | tf_op jit(solution)/shard_map/hidden/pallas_call | solution.py:77
  234.0 12.7 %expert.10 = (bf16[160,1024]{1,0:T(8,128)(2,1)S(1)}, f32[16,1024]{1,0:T(8,128)S(1)}) custom-call(s32[2]{0:T(128)S(1)} %copy-done.22, bf16[3,160,1152]{2,1,0:T(8,128)(2,1)S(1)} %maximum_maximum_fusion.u_ref, bf16[160,1024]{1,0:T(8,128)(2,1)S(1)} %pad_maximum_fusion.10.grad_ref, bf16[160,4096]{1,0:T(8,128)(2,1)S(1)} %copy-done.10, ...), custom_call_target="tpu_custom_call" | custom-call | flops 2684354560 | bytes 16777216 | tf_op jit(solution)/shard_map/expert/pallas_call | solution.py:153
  254.0 2.2 token_.10
  258.5 5.5 %collective-permute-done.39.in_ref = bf16[64,1024]{1,0:T(8,128)(2,1)S(1)} collective-permute-done((bf16[64,1024]{1,0:T(8,128)(2,1)}, bf16[64,1024]{1,0:T(8,128)(2,1)S(1)}, u32[]{:S(2)}, u32[]{:S(2)}) %collective-permute-start.39) | collective-permute-done | bytes 131104 | tf_op jit(solution)/shard_map/ppermute | solution.py:333
  274.1 2.5 collective-permute-done.40
  278.9 12.7 %expert.11 = (bf16[160,1024]{1,0:T(8,128)(2,1)S(1)}, f32[16,1024]{1,0:T(8,128)S(1)}) custom-call(s32[2]{0:T(128)S(1)} %copy-done.20, bf16[3,160,1152]{2,1,0:T(8,128)(2,1)S(1)} %maximum_maximum_fusion.u_ref, bf16[160,1024]{1,0:T(8,128)(2,1)S(1)} %pad_maximum_fusion.12.grad_ref, bf16[160,4096]{1,0:T(8,128)(2,1)S(1)} %get-tuple-element.77.active_ref, ...), custom_call_target="tpu_custom_call" | custom-call | flops 2684354560 | bytes 16777216 | tf_op jit(solution)/shard_map/expert/pallas_call | solution.py:153
  (313 shorter events, 135.8 us)
Async XLA Ops:
  7.6 9.2 %collective-permute-start.2 = (bf16[40,2176]{1,0:T(8,128)(2,1)S(1)}, bf16[40,2176]{1,0:T(8,128)(2,1)S(1)}, u32[]{:S(2)}, u32[]{:S(2)}) collective-permute-start(bf16[40,2176]{1,0:T(8,128)(2,1)S(1)} %get-tuple-element.99), channel_id=1, source_target_pairs={{0,6},{2,4},{4,2},{6,0},{1,7},{3,5},{5,3},{7,1},{8,14},{10,12},{12... | collective-permute-start | bytes 522248 | tf_op jit(solution)/shard_map/ppermute | solution.py:37
  11.5 8.2 %collective-permute-start.1 = (bf16[40,2176]{1,0:T(8,128)(2,1)S(1)}, bf16[40,2176]{1,0:T(8,128)(2,1)S(1)}, u32[]{:S(2)}, u32[]{:S(2)}) collective-permute-start(bf16[40,2176]{1,0:T(8,128)(2,1)S(1)} %get-tuple-element.100), channel_id=1, source_target_pairs={{0,4},{2,6},{4,0},{6,2},{1,5},{3,7},{5,1},{7,3},{8,12},{10,14},{12... | collective-permute-start | bytes 522248 | tf_op jit(solution)/shard_map/ppermute | solution.py:37
  12.0 9.5 %collective-permute-start = (bf16[40,2176]{1,0:T(8,128)(2,1)S(1)}, bf16[40,2176]{1,0:T(8,128)(2,1)S(1)}, u32[]{:S(2)}, u32[]{:S(2)}) collective-permute-start(bf16[40,2176]{1,0:T(8,128)(2,1)S(1)} %get-tuple-element.101), channel_id=1, source_target_pairs={{0,2},{2,0},{4,6},{6,4},{1,3},{3,1},{5,7},{7,5},{8,10},{10,8},{12,... | collective-permute-start | bytes 522248 | tf_op jit(solution)/shard_map/ppermute | solution.py:37
  12.2 9.5 %collective-permute-start.3 = (bf16[1024,2048]{1,0:T(8,128)(2,1)}, bf16[1024,2048]{1,0:T(8,128)(2,1)}, u32[]{:S(2)}, u32[]{:S(2)}) collective-permute-start(bf16[1024,2048]{1,0:T(8,128)(2,1)} %bitcast.190), channel_id=1, source_target_pairs={{0,1},{1,0},{2,3},{3,2},{4,5},{5,4},{6,7},{7,6},{8,9},{9,8},{10,11... | collective-permute-start | bytes 12582920 | tf_op jit(solution)/shard_map/ppermute | solution.py:265
  12.2 17.3 %collective-permute-start.4 = (bf16[2048,1024]{1,0:T(8,128)(2,1)}, bf16[2048,1024]{1,0:T(8,128)(2,1)}, u32[]{:S(2)}, u32[]{:S(2)}) collective-permute-start(bf16[2048,1024]{1,0:T(8,128)(2,1)} %bitcast.209), channel_id=1, source_target_pairs={{0,1},{1,0},{2,3},{3,2},{4,5},{5,4},{6,7},{7,6},{8,9},{9,8},{10,11... | collective-permute-start | bytes 12582920 | tf_op jit(solution)/shard_map/ppermute | solution.py:268
  16.8 40.5 %collective-permute-start.10 = (bf16[2,40,1152]{2,1,0:T(8,128)(2,1)S(1)}, bf16[2,40,1152]{2,1,0:T(8,128)(2,1)S(1)}, u32[]{:S(2)}, u32[]{:S(2)}) collective-permute-start(bf16[2,40,1152]{2,1,0:T(8,128)(2,1)S(1)} %pad_maximum_fusion.16), channel_id=1, source_target_pairs={{0,6},{2,4},{4,2},{6,0},{1,7},{3,5},{5,3},{7,1},{8,14},{10,12},{12... | collective-permute-start | bytes 552968 | tf_op jit(solution)/shard_map/ppermute | solution.py:37
  19.8 37.5 %collective-permute-start.9 = (bf16[2,40,1152]{2,1,0:T(8,128)(2,1)S(1)}, bf16[2,40,1152]{2,1,0:T(8,128)(2,1)S(1)}, u32[]{:S(2)}, u32[]{:S(2)}) collective-permute-start(bf16[2,40,1152]{2,1,0:T(8,128)(2,1)S(1)} %pad_maximum_fusion.15), channel_id=1, source_target_pairs={{0,4},{2,6},{4,0},{6,2},{1,5},{3,7},{5,1},{7,3},{8,12},{10,14},{12... | collective-permute-start | bytes 552968 | tf_op jit(solution)/shard_map/ppermute | solution.py:37
  42.2 6.3 %collective-permute-start.7 = (bf16[40,1024]{1,0:T(8,128)(2,1)S(1)}, bf16[40,1024]{1,0:T(8,128)(2,1)S(1)}, u32[]{:S(2)}, u32[]{:S(2)}) collective-permute-start(bf16[40,1024]{1,0:T(8,128)(2,1)S(1)} %get-tuple-element.151), channel_id=1, source_target_pairs={{6,0},{4,2},{2,4},{0,6},{7,1},{5,3},{3,5},{1,7},{14,8},{12,10},{10... | collective-permute-start | bytes 245768 | tf_op jit(solution)/shard_map/ppermute | solution.py:37
  43.7 13.5 %collective-permute-start.8 = (bf16[2,40,1152]{2,1,0:T(8,128)(2,1)S(1)}, bf16[2,40,1152]{2,1,0:T(8,128)(2,1)S(1)}, u32[]{:S(2)}, u32[]{:S(2)}) collective-permute-start(bf16[2,40,1152]{2,1,0:T(8,128)(2,1)S(1)} %pad_maximum_fusion.14), channel_id=1, source_target_pairs={{0,2},{2,0},{4,6},{6,4},{1,3},{3,1},{5,7},{7,5},{8,10},{10,8},{12,... | collective-permute-start | bytes 552968 | tf_op jit(solution)/shard_map/ppermute | solution.py:37
  55.9 7.1 %collective-permute-start.11 = (bf16[64,1024]{1,0:T(8,128)(2,1)}, bf16[64,1024]{1,0:T(8,128)(2,1)S(1)}, u32[]{:S(2)}, u32[]{:S(2)}) collective-permute-start(bf16[64,1024]{1,0:T(8,128)(2,1)} %token_.6), channel_id=1, source_target_pairs={{8,0},{16,8},{24,16},{9,1},{17,9},{25,17},{10,2},{18,10},{26,18},{... | collective-permute-start | bytes 393224 | tf_op jit(solution)/shard_map/ppermute | solution.py:333
  66.7 13.5 %collective-permute-start.14 = (bf16[40,1024]{1,0:T(8,128)(2,1)S(1)}, bf16[40,1024]{1,0:T(8,128)(2,1)S(1)}, u32[]{:S(2)}, u32[]{:S(2)}) collective-permute-start(bf16[40,1024]{1,0:T(8,128)(2,1)S(1)} %get-tuple-element.147), channel_id=1, source_target_pairs={{0,6},{2,4},{4,2},{6,0},{1,7},{3,5},{5,3},{7,1},{8,14},{10,12},{12... | collective-permute-start | bytes 245768 | tf_op jit(solution)/shard_map/ppermute | solution.py:37
  68.2 12.0 %collective-permute-start.13 = (bf16[40,1024]{1,0:T(8,128)(2,1)S(1)}, bf16[40,1024]{1,0:T(8,128)(2,1)S(1)}, u32[]{:S(2)}, u32[]{:S(2)}) collective-permute-start(bf16[40,1024]{1,0:T(8,128)(2,1)S(1)} %get-tuple-element.148), channel_id=1, source_target_pairs={{0,4},{2,6},{4,0},{6,2},{1,5},{3,7},{5,1},{7,3},{8,12},{10,14},{12... | collective-permute-start | bytes 245768 | tf_op jit(solution)/shard_map/ppermute | solution.py:37
  68.8 11.5 %collective-permute-start.12 = (bf16[40,1024]{1,0:T(8,128)(2,1)S(1)}, bf16[40,1024]{1,0:T(8,128)(2,1)S(1)}, u32[]{:S(2)}, u32[]{:S(2)}) collective-permute-start(bf16[40,1024]{1,0:T(8,128)(2,1)S(1)} %get-tuple-element.149), channel_id=1, source_target_pairs={{0,2},{2,0},{4,6},{6,4},{1,3},{3,1},{5,7},{7,5},{8,10},{10,8},{12,... | collective-permute-start | bytes 245768 | tf_op jit(solution)/shard_map/ppermute | solution.py:37
  102.5 7.1 %collective-permute-start.18 = (bf16[64,1024]{1,0:T(8,128)(2,1)}, bf16[64,1024]{1,0:T(8,128)(2,1)S(1)}, u32[]{:S(2)}, u32[]{:S(2)}) collective-permute-start(bf16[64,1024]{1,0:T(8,128)(2,1)} %token_.7), channel_id=1, source_target_pairs={{8,0},{16,8},{24,16},{9,1},{17,9},{25,17},{10,2},{18,10},{26,18},{... | collective-permute-start | bytes 393224 | tf_op jit(solution)/shard_map/ppermute | solution.py:333
  113.3 14.2 %collective-permute-start.21 = (bf16[40,1024]{1,0:T(8,128)(2,1)S(1)}, bf16[40,1024]{1,0:T(8,128)(2,1)S(1)}, u32[]{:S(2)}, u32[]{:S(2)}) collective-permute-start(bf16[40,1024]{1,0:T(8,128)(2,1)S(1)} %get-tuple-element.139), channel_id=1, source_target_pairs={{0,6},{2,4},{4,2},{6,0},{1,7},{3,5},{5,3},{7,1},{8,14},{10,12},{12... | collective-permute-start | bytes 245768 | tf_op jit(solution)/shard_map/ppermute | solution.py:37
  114.8 12.7 %collective-permute-start.20 = (bf16[40,1024]{1,0:T(8,128)(2,1)S(1)}, bf16[40,1024]{1,0:T(8,128)(2,1)S(1)}, u32[]{:S(2)}, u32[]{:S(2)}) collective-permute-start(bf16[40,1024]{1,0:T(8,128)(2,1)S(1)} %get-tuple-element.140), channel_id=1, source_target_pairs={{0,4},{2,6},{4,0},{6,2},{1,5},{3,7},{5,1},{7,3},{8,12},{10,14},{12... | collective-permute-start | bytes 245768 | tf_op jit(solution)/shard_map/ppermute | solution.py:37
  116.3 11.2 %collective-permute-start.19 = (bf16[40,1024]{1,0:T(8,128)(2,1)S(1)}, bf16[40,1024]{1,0:T(8,128)(2,1)S(1)}, u32[]{:S(2)}, u32[]{:S(2)}) collective-permute-start(bf16[40,1024]{1,0:T(8,128)(2,1)S(1)} %get-tuple-element.141), channel_id=1, source_target_pairs={{0,2},{2,0},{4,6},{6,4},{1,3},{3,1},{5,7},{7,5},{8,10},{10,8},{12,... | collective-permute-start | bytes 245768 | tf_op jit(solution)/shard_map/ppermute | solution.py:37
  150.7 7.1 %collective-permute-start.25 = (bf16[64,1024]{1,0:T(8,128)(2,1)}, bf16[64,1024]{1,0:T(8,128)(2,1)S(1)}, u32[]{:S(2)}, u32[]{:S(2)}) collective-permute-start(bf16[64,1024]{1,0:T(8,128)(2,1)} %token_.8), channel_id=1, source_target_pairs={{8,0},{16,8},{24,16},{9,1},{17,9},{25,17},{10,2},{18,10},{26,18},{... | collective-permute-start | bytes 393224 | tf_op jit(solution)/shard_map/ppermute | solution.py:333
  161.5 14.1 %collective-permute-start.28 = (bf16[40,1024]{1,0:T(8,128)(2,1)S(1)}, bf16[40,1024]{1,0:T(8,128)(2,1)S(1)}, u32[]{:S(2)}, u32[]{:S(2)}) collective-permute-start(bf16[40,1024]{1,0:T(8,128)(2,1)S(1)} %get-tuple-element.131), channel_id=1, source_target_pairs={{0,6},{2,4},{4,2},{6,0},{1,7},{3,5},{5,3},{7,1},{8,14},{10,12},{12... | collective-permute-start | bytes 245768 | tf_op jit(solution)/shard_map/ppermute | solution.py:37
  163.0 12.7 %collective-permute-start.27 = (bf16[40,1024]{1,0:T(8,128)(2,1)S(1)}, bf16[40,1024]{1,0:T(8,128)(2,1)S(1)}, u32[]{:S(2)}, u32[]{:S(2)}) collective-permute-start(bf16[40,1024]{1,0:T(8,128)(2,1)S(1)} %get-tuple-element.132), channel_id=1, source_target_pairs={{0,4},{2,6},{4,0},{6,2},{1,5},{3,7},{5,1},{7,3},{8,12},{10,14},{12... | collective-permute-start | bytes 245768 | tf_op jit(solution)/shard_map/ppermute | solution.py:37
  163.5 12.1 %collective-permute-start.26 = (bf16[40,1024]{1,0:T(8,128)(2,1)S(1)}, bf16[40,1024]{1,0:T(8,128)(2,1)S(1)}, u32[]{:S(2)}, u32[]{:S(2)}) collective-permute-start(bf16[40,1024]{1,0:T(8,128)(2,1)S(1)} %get-tuple-element.133), channel_id=1, source_target_pairs={{0,2},{2,0},{4,6},{6,4},{1,3},{3,1},{5,7},{7,5},{8,10},{10,8},{12,... | collective-permute-start | bytes 245768 | tf_op jit(solution)/shard_map/ppermute | solution.py:37
  197.9 21.2 %collective-permute-start.32 = (bf16[64,1024]{1,0:T(8,128)(2,1)}, bf16[64,1024]{1,0:T(8,128)(2,1)S(1)}, u32[]{:S(2)}, u32[]{:S(2)}) collective-permute-start(bf16[64,1024]{1,0:T(8,128)(2,1)} %token_.9), channel_id=1, source_target_pairs={{8,0},{16,8},{24,16},{9,1},{17,9},{25,17},{10,2},{18,10},{26,18},{... | collective-permute-start | bytes 393224 | tf_op jit(solution)/shard_map/ppermute | solution.py:333
  256.2 7.8 %collective-permute-start.39 = (bf16[64,1024]{1,0:T(8,128)(2,1)}, bf16[64,1024]{1,0:T(8,128)(2,1)S(1)}, u32[]{:S(2)}, u32[]{:S(2)}) collective-permute-start(bf16[64,1024]{1,0:T(8,128)(2,1)} %token_.10), channel_id=1, source_target_pairs={{8,0},{16,8},{24,16},{9,1},{17,9},{25,17},{10,2},{18,10},{26,18},{... | collective-permute-start | bytes 393224 | tf_op jit(solution)/shard_map/ppermute | solution.py:333
  291.7 5.6 %collective-permute-start.45 = (bf16[48,1024]{1,0:T(8,128)(2,1)S(1)}, bf16[48,1024]{1,0:T(8,128)(2,1)S(1)}, u32[]{:S(2)}, u32[]{:S(2)}) collective-permute-start(bf16[48,1024]{1,0:T(8,128)(2,1)S(1)} %get-tuple-element.162), channel_id=1, source_target_pairs={{6,0},{4,2},{2,4},{0,6},{7,1},{5,3},{3,5},{1,7},{14,8},{12,10},{10... | collective-permute-start | bytes 294920 | tf_op jit(solution)/shard_map/ppermute | solution.py:37
  (71 other events, 495.0 us)
